TPU v7x, 32 devices: a whole 2x2x4 slice. The times are simulated.
32 devices in a mesh: section: 4 (over z), head: 2 (over y), key: 4 (over x, core).
Axes of the slice: x: 2, y: 2, z: 4, core: 2. Of those that a mesh axis runs over, the one named last changes fastest.
Arguments:
- queries: bfloat16 [4, 256, 3072], P('section', None, 'head'), may hold values from -1024 to 1024
- attn_grad: bfloat16 [4, 256, 3072], P('section', None, 'head'), may hold values from -192 to 192
- query_weight: bfloat16 [4, 3072, 3072], P('section', None, 'head'), may hold values from -0.109375 to 0.109375
- key_codes: int32 [4096, 1024], P('key', 'head'), may hold values from -127 to 127
- key_exps: int32 [64, 8], P('key', 'head'), may hold values from -9 to -6
- value_codes: int32 [4096, 1024], P('key', 'head'), may hold values from -127 to 127
- value_exps: int32 [64, 8], P('key', 'head'), may hold values from -9 to -6
Outputs:
- input_grad: bfloat16 [4, 256, 3072], P('section', ('head', 'key'))
- key_grad: float32 [4096, 1024], P(('key', 'section'), 'head')
- value_grad: float32 [4096, 1024], P(('key', 'section'), 'head')
All inputs are finite; a program needn't handle non-finite values.
Results may differ from a plain program's by a relative error of at most 0.017.
Values may be sent and summed in bfloat16 or wider, within the bound.
A program may use at most 128 MiB of HBM per device.

v0:
```python
from functools import reduce

import jax
import jax.numpy as jnp
from jax import lax
from jax.sharding import PartitionSpec as P

HQ = 24
KVH = 8
HD = 128
TICKS = 2
TICK_ROWS = 128
ROWS = 256


def combined_all(value, axis, join):
    pieces = jax.tree.map(lambda part: lax.all_gather(part, axis), value)
    head = jax.tree.map(lambda part: part[0], pieces)
    tail = jax.tree.map(lambda part: part[1:], pieces)
    total, _ = lax.scan(lambda total, slab: (join(total, slab), None), head, tail)
    return total


def dequantize(code_array, exponents):
    row_count = code_array.shape[0]
    kv_local = exponents.shape[1]
    factor = jnp.exp2(exponents.astype(jnp.float32))
    factor = jnp.repeat(factor, row_count // exponents.shape[0], axis=0)
    shaped = code_array.astype(jnp.float32).reshape(row_count, kv_local, HD)
    return (shaped * factor[:, :, None]).astype(jnp.bfloat16)


def merge_stats(earlier, later):
    peak_value = jnp.maximum(earlier[0], later[0])
    weight_early = jnp.exp(earlier[0] - peak_value)
    weight_late = jnp.exp(later[0] - peak_value)
    return (peak_value, earlier[1] * weight_early + later[1] * weight_late)


def body(queries, attn_grad, query_weight, key_codes, key_exps, value_codes, value_exps):
    key_vals = dequantize(key_codes, key_exps)
    value_vals = dequantize(value_codes, value_exps)
    key_rows = key_vals.shape[0]
    kv_local = key_vals.shape[1]
    group_size = HQ // KVH
    score_scale = HD ** (-0.5)
    query_rows = queries[0]
    grad_rows = attn_grad[0]
    head_cols = query_rows.shape[1]
    query_ticks = []
    key_parts = []
    value_parts = []
    for tick_index in range(TICKS):
        first_row = tick_index * TICK_ROWS
        query_tick = query_rows[first_row : first_row + TICK_ROWS].reshape(
            TICK_ROWS, kv_local, group_size, HD
        )
        grad_tick = grad_rows[first_row : first_row + TICK_ROWS].reshape(
            TICK_ROWS, kv_local, group_size, HD
        )
        scores = (
            jnp.einsum("rkgd,skd->kgrs", query_tick, key_vals, preferred_element_type=jnp.float32)
            * score_scale
        )
        grad_probs = jnp.einsum(
            "rkgd,skd->kgrs", grad_tick, value_vals, preferred_element_type=jnp.float32
        )
        row_max = jnp.max(scores, axis=-1)
        shifted = jnp.exp(scores - row_max[..., None])
        row_total = jnp.sum(shifted, axis=-1)
        max_all, total_all = combined_all((row_max, row_total), "key", merge_stats)
        prob_full = jnp.exp(scores - max_all[..., None]) / total_all[..., None]
        row_delta = lax.psum(jnp.sum(prob_full * grad_probs, axis=-1), "key")
        grad_scores = prob_full * (grad_probs - row_delta[..., None])
        probs_low = prob_full.astype(jnp.bfloat16)
        grads_low = grad_scores.astype(jnp.bfloat16)
        key_part = (
            jnp.einsum("kgrs,rkgd->skd", grads_low, query_tick, preferred_element_type=jnp.float32)
            * score_scale
        )
        key_part = key_part.reshape(key_rows, kv_local * HD)
        value_part = jnp.einsum(
            "kgrs,rkgd->skd", probs_low, grad_tick, preferred_element_type=jnp.float32
        )
        value_part = value_part.reshape(key_rows, kv_local * HD)
        query_part = (
            jnp.einsum("kgrs,skd->rkgd", grads_low, key_vals, preferred_element_type=jnp.float32)
            * score_scale
        )
        query_ticks.append(query_part.reshape(TICK_ROWS, head_cols))
        key_piece, value_piece = (
            lax.psum_scatter(
                key_part.astype(jnp.bfloat16), "section", scatter_dimension=0, tiled=True
            ).astype(jnp.float32),
            lax.psum_scatter(
                value_part.astype(jnp.bfloat16), "section", scatter_dimension=0, tiled=True
            ).astype(jnp.float32),
        )
        key_parts.append(key_piece)
        value_parts.append(value_piece)
    key_total = reduce(jnp.add, key_parts)
    value_total = reduce(jnp.add, value_parts)
    query_grad = jnp.concatenate(query_ticks, axis=0)
    head_count = lax.axis_size("head")
    key_count = lax.axis_size("key")
    block_rows = ROWS // (head_count * key_count)
    query_blocks = query_grad.reshape(head_count, key_count, block_rows, head_cols)
    query_summed = lax.psum_scatter(
        query_blocks.astype(jnp.bfloat16), "key", scatter_dimension=1, tiled=True
    ).astype(jnp.float32)
    query_low = query_summed.reshape(head_count * block_rows, head_cols).astype(jnp.bfloat16)
    weight_local = query_weight[0]
    input_part = lax.psum_scatter(
        lax.dot_general(
            query_low, weight_local, (((1,), (1,)), ((), ())), preferred_element_type=jnp.float32
        ).astype(jnp.bfloat16),
        "head",
        scatter_dimension=0,
        tiled=True,
    )
    input_grad = input_part.reshape(1, block_rows, weight_local.shape[0])
    return (input_grad, key_total, value_total)


def solution(mesh):
    return jax.shard_map(
        body,
        mesh=mesh,
        in_specs=(
            P("section", None, "head"),
            P("section", None, "head"),
            P("section", None, "head"),
            P("key", "head"),
            P("key", "head"),
            P("key", "head"),
            P("key", "head"),
        ),
        out_specs=(
            P("section", ("head", "key"), None),
            P(("key", "section"), "head"),
            P(("key", "section"), "head"),
        ),
        check_vma=False,
    )
```

profile of v0, /device:TPU:0, one launch (start us, length us, event | category | flops | bytes accessed | tf_op | source)
XLA Modules:
  0.0 237.2 jit_solution(2584146881427336091)
XLA Ops:
  8.1 3.2 %convert_element_type.90 = f32[1024,512]{1,0:T(8,128)} convert(s32[1024,512]{1,0:T(8,128)} %param.14) | non-fusion elementwise | flops 524288 | bytes 4194304 | tf_op jit(solution)/shard_map/convert_element_type | solution.py:29
  15.7 2.6 %copy-done = f32[4,1024,128,3]{2,1,3,0:T(8,128)} copy-done((f32[4,1024,128,3]{2,1,3,0:T(8,128)}, f32[4,1024,128,3]{2,1,3,0:T(8,128)S(1)}, u32[]{:S(2)}) %copy-start) | copy-done | bytes 6291480
  19.4 6.2 %all-gather.1 = f32[16,3,128]{2,1,0:T(4,128)S(1)} all-gather(f32[4,3,128]{2,1,0:T(4,128)S(1)} %fusion.17), channel_id=3, replica_groups=mesh['section'=4,'head'=2,'key'=4] {'key'}, dimensions={0}, use_global_device_ids=true | all-gather | bytes 30720 | tf_op jit(solution)/shard_map/all_gather | solution.py:17
  25.6 5.4 %all-gather = f32[16,3,128]{2,1,0:T(4,128)S(1)} all-gather(f32[4,3,128]{2,1,0:T(4,128)S(1)} %get-tuple-element.97), channel_id=2, replica_groups=mesh['section'=4,'head'=2,'key'=4] {'key'}, dimensions={0}, use_global_device_ids=true | all-gather | bytes 30720 | tf_op jit(solution)/shard_map/all_gather | solution.py:17
  32.3 2.6 %copy-done.1 = f32[4,1024,128,3]{2,1,3,0:T(8,128)} copy-done((f32[4,1024,128,3]{2,1,3,0:T(8,128)}, f32[4,1024,128,3]{2,1,3,0:T(8,128)S(1)}, u32[]{:S(2)}) %copy-start.1) | copy-done | bytes 6291480
  36.0 5.2 %all-gather.3 = f32[16,3,128]{2,1,0:T(4,128)S(1)} all-gather(f32[4,3,128]{2,1,0:T(4,128)S(1)} %fusion.10), channel_id=5, replica_groups=mesh['section'=4,'head'=2,'key'=4] {'key'}, dimensions={0}, use_global_device_ids=true | all-gather | bytes 30720 | tf_op jit(solution)/shard_map/all_gather | solution.py:17
  41.2 5.2 %all-gather.2 = f32[16,3,128]{2,1,0:T(4,128)S(1)} all-gather(f32[4,3,128]{2,1,0:T(4,128)S(1)} %get-tuple-element.93), channel_id=4, replica_groups=mesh['section'=4,'head'=2,'key'=4] {'key'}, dimensions={0}, use_global_device_ids=true | all-gather | bytes 30720 | tf_op jit(solution)/shard_map/all_gather | solution.py:17
  53.4 7.2 %fusion.13 = (f32[4,3,128]{2,1,0:T(4,128)}, f32[4,1024,128,3]{2,1,3,0:T(8,128)}) fusion(f32[4,3,128]{2,1,0:T(4,128)} %copy-done.7, f32[4,3,128]{2,1,0:T(4,128)} %copy-done.9, f32[4,1024,128,3]{2,1,3,0:T(8,128)} %copy-done, bf16[128,4,3,128]{0,3,2,1:T(8,128)(2,1)} %bitcast.214, f32[1024,4]{0,1:T(4,128)} %mul.81, s32[1024,512]{1,0:T(8,128)} %param.16), kind=kOutput, calls=%fused_computation.26 | convolution fusion | flops 412088832 | bytes 15108096 | tf_op jit(solution)/shard_map/rkgd,skd->kgrs/dot_general | solution.py:65
  61.3 4.8 %fusion.6 = (f32[4,3,128]{2,1,0:T(4,128)}, f32[4,1024,128,3]{2,1,3,0:T(8,128)}) fusion(f32[4,3,128]{2,1,0:T(4,128)S(1)} %get-tuple-element.62, f32[4,3,128]{2,1,0:T(4,128)S(1)} %get-tuple-element.61, f32[4,1024,128,3]{2,1,3,0:T(8,128)S(1)} %bitcast.200, bf16[128,4,3,128]{0,3,2,1:T(8,128)(2,1)S(1)} %bitcast.216, f32[1024,4]{0,1:T(4,128)S(1)} %copy-done.14, ...), kind=kOutput, calls=%fused_computation.14 | convolution fusion | flops 412088832 | bytes 15108096 | tf_op jit(solution)/shard_map/rkgd,skd->kgrs/dot_general | solution.py:65
  66.0 12.3 %all-reduce.1 = (f32[4,3,128]{2,1,0:T(4,128)S(1)}, f32[4,3,128]{2,1,0:T(4,128)S(1)}) all-reduce(f32[4,3,128]{2,1,0:T(4,128)} %get-tuple-element.95, f32[4,3,128]{2,1,0:T(4,128)} %get-tuple-element.99), channel_id=1, replica_groups=mesh['section'=4,'head'=2,'key'=4] {'key'}, use_global_device_ids=true, to_apply=%region_11.12 | all-reduce | flops 3072 | bytes 24576 | tf_op jit(solution)/shard_map/psum | solution.py:73
  78.3 12.8 %fusion.8 = (bf16[4,3,128,1024]{2,3,1,0:T(8,128)(2,1)}, bf16[4,3,128,1024]{2,3,1,0:T(8,128)(2,1)}) fusion(f32[4,1024,128,3]{2,1,3,0:T(8,128)} %get-tuple-element.96, f32[4,3,128]{2,1,0:T(4,128)S(1)} %get-tuple-element.83, f32[4,3,128]{2,1,0:T(4,128)S(1)} %get-tuple-element.62, f32[4,3,128]{2,1,0:T(4,128)S(1)} %get-tuple-element.61, ...), kind=kLoop, calls=%fused_computation.16 | loop fusion | flops 18874368 | bytes 31494144 | tf_op jit(solution)/shard_map/convert_element_type | solution.py:76
  91.1 2.6 %fusion.34 = bf16[4,128,3,128]{3,1,2,0:T(8,128)(2,1)S(1)} fusion(bf16[1024,4,128,1]{0,2,3,1:T(8,128)(2,1)S(1)} %fusion.36, bf16[4,3,128,1024]{2,3,1,0:T(8,128)(2,1)} %get-tuple-element.102), kind=kOutput, calls=%fused_computation.53 | convolution fusion | flops 403046400 | bytes 4587520 | tf_op jit(solution)/shard_map/kgrs,skd->rkgd/dot_general | solution.py:87
  93.9 2.6 %fusion.35 = bf16[4,128,3,128]{3,1,2,0:T(8,128)(2,1)S(1)} fusion(bf16[1024,4,128,1]{0,2,3,1:T(8,128)(2,1)S(1)} %fusion.36, bf16[4,3,128,1024]{2,3,1,0:T(8,128)(2,1)} %get-tuple-element.101), kind=kOutput, calls=%fused_computation.54 | convolution fusion | flops 403046400 | bytes 4587520 | tf_op jit(solution)/shard_map/kgrs,skd->rkgd/dot_general | solution.py:87
  97.8 4.4 %bitcast_convert_fusion.1 = bf16[4,1024,128]{1,2,0:T(8,128)(2,1)S(1)} fusion(bf16[128,4,3,128]{0,3,2,1:T(8,128)(2,1)S(1)} %bitcast.215, f32[4,1024,128,3]{2,1,3,0:T(8,128)} %copy-done, f32[4,3,128]{2,1,0:T(4,128)S(1)} %copy-done.8, f32[4,3,128]{2,1,0:T(4,128)S(1)} %copy-done.10), kind=kOutput, calls=%fused_computation.44 | convolution fusion | flops 409468928 | bytes 7745536 | tf_op jit(solution)/shard_map/kgrs,rkgd->skd/dot_general | solution.py:82
  103.6 5.4 %bitcast_convert_fusion = bf16[4,1024,128]{1,2,0:T(8,128)(2,1)} fusion(bf16[128,4,3,128]{0,3,2,1:T(8,128)(2,1)S(1)} %bitcast.217, f32[4,1024,128,3]{2,1,3,0:T(8,128)} %copy-done.1, f32[4,3,128]{2,1,0:T(4,128)S(1)} %get-tuple-element.62, f32[4,3,128]{2,1,0:T(4,128)S(1)} %get-tuple-element.61), kind=kOutput, calls=%fused_computation.43 | convolution fusion | flops 409468928 | bytes 7745536 | tf_op jit(solution)/shard_map/kgrs,rkgd->skd/dot_general | solution.py:82
  109.0 2.5 %copy.75 = bf16[1024,512]{1,0:T(8,128)(2,1)} copy(bf16[1024,512]{0,1:T(8,128)(2,1)} %bitcast.210) | data formatting | bytes 2097152 | tf_op jit(solution)/shard_map/convert_element_type | solution.py:96
  111.6 4.0 %fusion.29 = bf16[4,1024,128]{1,2,0:T(8,128)(2,1)} fusion(bf16[4,3,128,1024]{2,3,1,0:T(8,128)(2,1)} %get-tuple-element.102, bf16[128,4,3,128]{0,3,2,1:T(8,128)(2,1)S(1)} %bitcast.204), kind=kOutput, calls=%fused_computation.48 | convolution fusion | flops 403701760 | bytes 4587520 | tf_op jit(solution)/shard_map/kgrs,rkgd->skd/dot_general | solution.py:78
  117.9 3.1 %fusion.28 = bf16[4,1024,128]{1,2,0:T(8,128)(2,1)} fusion(bf16[4,3,128,1024]{2,3,1,0:T(8,128)(2,1)S(1)} %copy-done.2, bf16[128,4,3,128]{0,3,2,1:T(8,128)(2,1)} %bitcast.206), kind=kOutput, calls=%fused_computation.46 | convolution fusion | flops 403701760 | bytes 4587520 | tf_op jit(solution)/shard_map/kgrs,rkgd->skd/dot_general | solution.py:78
  124.0 9.0 %all-reduce.4.cloned.1.call-done = bf16[2,4,32,1536]{3,2,1,0:T(8,128)(2,1)} async-done(((bf16[2,4,32,1536]{3,2,1,0:T(8,128)(2,1)}), bf16[2,4,32,1536]{3,2,1,0:T(8,128)(2,1)}) %all-reduce.4.cloned.1.call-update) | async-done | bytes 786448
  134.5 7.5 %fusion.20 = bf16[64,3072]{1,0:T(8,128)(2,1)} fusion(bf16[64,1536]{1,0:T(8,128)(2,1)S(1)} %bitcast.213, bf16[1,3072,1536]{2,1,0:T(8,128)(2,1)} %param.13), kind=kOutput, calls=%fused_computation.36 | convolution fusion | flops 604176384 | bytes 10027008 | tf_op jit(solution)/shard_map/dot_general | solution.py:114
  142.1 17.0 %reduce-scatter.17.cloned.1.call-done = bf16[256,512]{1,0:T(8,128)(2,1)} async-done(((bf16[1024,512]{1,0:T(8,128)(2,1)}), bf16[256,512]{1,0:T(8,128)(2,1)}) %reduce-scatter.17.cloned.1.call-update) | async-done | bytes 262160 | tf_op jit(solution)/shard_map/reduce_scatter | solution.py:95
  161.0 26.0 %reduce-scatter.11.cloned.1.call-done = bf16[256,512]{1,0:T(8,128)(2,1)} async-done(((bf16[1024,512]{1,0:T(8,128)(2,1)}), bf16[256,512]{1,0:T(8,128)(2,1)}) %reduce-scatter.11.cloned.1.call-update) | async-done | bytes 262160 | tf_op jit(solution)/shard_map/reduce_scatter | solution.py:92
  187.0 28.2 %reduce-scatter.13.cloned.1.call-done = bf16[256,512]{1,0:T(8,128)(2,1)} async-done(((bf16[1024,512]{1,0:T(8,128)(2,1)}), bf16[256,512]{1,0:T(8,128)(2,1)}) %reduce-scatter.13.cloned.1.call-update) | async-done | bytes 262160 | tf_op jit(solution)/shard_map/reduce_scatter | solution.py:92
  217.0 12.6 %reduce-scatter.9.cloned.1.call-done = bf16[32,3072]{1,0:T(8,128)(2,1)} async-done(((bf16[64,3072]{1,0:T(8,128)(2,1)}), bf16[32,3072]{1,0:T(8,128)(2,1)}) %reduce-scatter.9.cloned.1.call-update) | async-done | bytes 196624 | tf_op jit(solution)/shard_map/reduce_scatter | solution.py:113
  (96 shorter events, 29.2 us)
Async XLA Ops:
  8.0 5.2 %copy-start.15 = (s32[16,4]{0,1:T(4,128)S(1)}, s32[16,4]{0,1:T(4,128)}, u32[]{:S(2)}) copy-start(s32[16,4]{0,1:T(4,128)} %param.15) | copy-start | bytes 772
  8.0 5.4 %copy-start.5 = (bf16[1,256,1536]{2,1,0:T(8,128)(2,1)S(1)}, bf16[1,256,1536]{2,1,0:T(8,128)(2,1)}, u32[]{:S(2)}) copy-start(bf16[1,256,1536]{2,1,0:T(8,128)(2,1)} %param.11) | copy-start | bytes 2359300
  8.0 124.9 %all-reduce.4.cloned.1.call-start = ((), (), s32[]{:S(2)}) async-start(), calls=%async_computation.10 | async-start | bytes 1572864
  14.7 16.3 %copy-start.4 = (bf16[1,128,1536]{2,1,0:T(8,128)(2,1)S(1)}, bf16[1,128,1536]{2,1,0:T(8,128)(2,1)}, u32[]{:S(2)}) copy-start(bf16[1,128,1536]{2,1,0:T(8,128)(2,1)} %get-tuple-element.90) | copy-start | bytes 1179652
  15.7 2.6 %copy-start = (f32[4,1024,128,3]{2,1,3,0:T(8,128)}, f32[4,1024,128,3]{2,1,3,0:T(8,128)S(1)}, u32[]{:S(2)}) copy-start(f32[4,1024,128,3]{2,1,3,0:T(8,128)S(1)} %get-tuple-element.98) | copy-start | bytes 18874372
  31.2 4.7 %copy-start.3 = (bf16[1,128,1536]{1,2,0:T(8,128)(2,1)}, bf16[1,128,1536]{1,2,0:T(8,128)(2,1)S(1)}, u32[]{:S(2)}) copy-start(bf16[1,128,1536]{1,2,0:T(8,128)(2,1)S(1)} %copy.103) | copy-start | bytes 1179652
  32.3 2.6 %copy-start.1 = (f32[4,1024,128,3]{2,1,3,0:T(8,128)}, f32[4,1024,128,3]{2,1,3,0:T(8,128)S(1)}, u32[]{:S(2)}) copy-start(f32[4,1024,128,3]{2,1,3,0:T(8,128)S(1)} %get-tuple-element.94) | copy-start | bytes 18874372
  32.3 14.2 %copy-start.6 = (bf16[1,256,1536]{2,1,0:T(8,128)(2,1)S(1)}, bf16[1,256,1536]{2,1,0:T(8,128)(2,1)}, u32[]{:S(2)}) copy-start(bf16[1,256,1536]{2,1,0:T(8,128)(2,1)} %param.12) | copy-start | bytes 2359300
  48.5 12.1 %slice-start = ((s8[6291456]{0:T(1024)(128)(4,1)}), s8[2097152]{0:T(1024)(128)(4,1)S(1)}, s32[]{:S(2)}) async-start(s8[6291456]{0:T(1024)(128)(4,1)} %bitcast.199), calls=%async_computation.11 | async-start | bytes 4194304
  53.4 7.2 %slice-start.1 = ((s8[6291456]{0:T(1024)(128)(4,1)}), s8[4194304]{0:T(1024)(128)(4,1)S(1)}, s32[]{:S(2)}) async-start(s8[6291456]{0:T(1024)(128)(4,1)} %bitcast.199), calls=%async_computation.12 | async-start | bytes 8388608
  53.4 7.2 %copy-start.12 = (bf16[1,128,1536]{1,2,0:T(8,128)(2,1)S(1)}, bf16[1,128,1536]{1,2,0:T(8,128)(2,1)}, u32[]{:S(2)}) copy-start(bf16[1,128,1536]{1,2,0:T(8,128)(2,1)} %copy.104) | copy-start | bytes 1179652
  53.4 7.2 %copy-start.14 = (f32[1024,4]{0,1:T(4,128)S(1)}, f32[1024,4]{0,1:T(4,128)}, u32[]{:S(2)}) copy-start(f32[1024,4]{0,1:T(4,128)} %mul.81) | copy-start | bytes 49156
  53.4 7.9 %copy-start.16 = (s32[1024,512]{1,0:T(8,128)S(1)}, s32[1024,512]{1,0:T(8,128)}, u32[]{:S(2)}) copy-start(s32[1024,512]{1,0:T(8,128)} %param.16) | copy-start | bytes 6291460
  91.1 6.7 %copy-start.8 = (f32[4,3,128]{2,1,0:T(4,128)S(1)}, f32[4,3,128]{2,1,0:T(4,128)}, u32[]{:S(2)}) copy-start(f32[4,3,128]{2,1,0:T(4,128)} %copy-done.7) | copy-start | bytes 18436
  91.1 6.7 %copy-start.10 = (f32[4,3,128]{2,1,0:T(4,128)S(1)}, f32[4,3,128]{2,1,0:T(4,128)}, u32[]{:S(2)}) copy-start(f32[4,3,128]{2,1,0:T(4,128)} %copy-done.9) | copy-start | bytes 18436
  91.1 6.7 %copy-start.11 = (bf16[1,128,1536]{1,2,0:T(8,128)(2,1)S(1)}, bf16[1,128,1536]{1,2,0:T(8,128)(2,1)}, u32[]{:S(2)}) copy-start(bf16[1,128,1536]{1,2,0:T(8,128)(2,1)} %copy.102) | copy-start | bytes 1179652
  97.7 5.9 %copy-start.13 = (bf16[1,128,1536]{1,2,0:T(8,128)(2,1)S(1)}, bf16[1,128,1536]{1,2,0:T(8,128)(2,1)}, u32[]{:S(2)}) copy-start(bf16[1,128,1536]{1,2,0:T(8,128)(2,1)} %copy.104) | copy-start | bytes 1179652
  97.7 44.4 %reduce-scatter.15.cloned.1.call-start = ((), (), s32[]{:S(2)}) async-start(), calls=%async_computation.8 | async-start | bytes 1310720 | tf_op jit(solution)/shard_map/reduce_scatter | solution.py:95
  103.5 55.6 %reduce-scatter.17.cloned.1.call-start = ((), (), s32[]{:S(2)}) async-start(), calls=%async_computation.9 | async-start | bytes 1310720 | tf_op jit(solution)/shard_map/reduce_scatter | solution.py:95
  109.0 8.9 %copy-start.2 = (bf16[4,3,128,1024]{2,3,1,0:T(8,128)(2,1)S(1)}, bf16[4,3,128,1024]{2,3,1,0:T(8,128)(2,1)}, u32[]{:S(2)}) copy-start(bf16[4,3,128,1024]{2,3,1,0:T(8,128)(2,1)} %get-tuple-element.101) | copy-start | bytes 9437188
  111.5 75.4 %reduce-scatter.11.cloned.1.call-start = ((), (), s32[]{:S(2)}) async-start(), calls=%async_computation.6 | async-start | bytes 1310720 | tf_op jit(solution)/shard_map/reduce_scatter | solution.py:92
  115.5 7.9 %copy-start.17 = (u32[32]{0:T(128)S(1)}, u32[32]{0:T(128)}, u32[]{:S(2)}) copy-start(u32[32]{0:T(128)} %constant.32) | copy-start | bytes 388
  117.9 97.3 %reduce-scatter.13.cloned.1.call-start = ((), (), s32[]{:S(2)}) async-start(), calls=%async_computation.7 | async-start | bytes 1310720 | tf_op jit(solution)/shard_map/reduce_scatter | solution.py:92
  123.3 106.2 %reduce-scatter.9.cloned.1.call-start = ((), (), s32[]{:S(2)}) async-start(), calls=%async_computation.5 | async-start | bytes 589824 | tf_op jit(solution)/shard_map/reduce_scatter | solution.py:113
  (2 other events, 3.8 us)
Sparse Core Ops, SparseCore 0:
  97.8 35.1 all-reduce.3
Sparse Core Ops, SparseCore 1:
  103.6 27.4 reduce-scatter.14
  133.4 25.7 reduce-scatter.16
  161.3 25.6 reduce-scatter.10
  189.4 25.7 reduce-scatter.12
  218.0 11.6 reduce-scatter.8
where the time goes:
time: 238 us; the launch traced here: 237 us
  waiting for transfers between devices  92.8 us (39%)
  matrix products  43.6 us (18%)
  blocking collectives  34.2 us (14%)
  local copies, waits for them, and re-layouts  26.3 us (11%)
  other arithmetic  23.9 us (10%)
  between operations  16 us (7%)
    reduce_scatter x2, waiting for transfers between devices, body(): lax.psum_scatter(key_part.astype(jnp.bfloat16), 'section', scatter_dimens...  54.1 us
    all_gather x4, blocking collectives, combined_all(): pieces = jax.tree.map(lambda part: lax.all_gather(part, axis), value)  22 us
    reduce_scatter x2, waiting for transfers between devices, body(): lax.psum_scatter(value_part.astype(jnp.bfloat16), 'section', scatter_dime...  17 us
    convert_element_type x1, other arithmetic, body(): grads_low = grad_scores.astype(jnp.bfloat16)  12.8 us
    reduce_scatter x1, waiting for transfers between devices, body(): lax.psum_scatter(lax.dot_general(query_low, weight_local, (((1,), (1,)),...  12.6 us
    psum x1, blocking collectives, body(): row_delta = lax.psum(jnp.sum(prob_full * grad_probs, axis=-1), 'key')  12.3 us
    dot_general x2, matrix products, body(): jnp.einsum('rkgd,skd->kgrs', grad_tick, value_vals, preferred_element_typ...  12 us
    unnamed x46, local copies, waits for them, and re-layouts  11.6 us
  transfers between devices with their start and end apart: 6, of which 5 were waited for; matrix products, arithmetic and copies ran while one was open for 16% of the time, Pallas kernels for 0%

commit v1 on v0

v1 whole, which is shorter than its diff:
```python
import functools

import jax
import jax.numpy as jnp
from jax import lax
from jax.experimental import pallas as pl
from jax.experimental.pallas import tpu as pltpu
from jax.sharding import PartitionSpec as P

HD = 128
LOG2E = 1.4426950408889634
MESH = pl.DeviceIdType.MESH
F32 = jnp.float32
BF16 = jnp.bfloat16
NT = (((1,), (1,)), ((), ()))
NN = (((1,), (0,)), ((), ()))
TN = (((0,), (0,)), ((), ()))


def dot(a, b, dims):
    return lax.dot_general(a, b, dims, preferred_element_type=F32)


def kernel(
    n_sec, n_head, n_key,
    q_hbm, do_hbm, w_hbm, kc_hbm, ke, vc_hbm, ve,
    in_out, key_out, value_out,
    q_v, do_v, w_v, kc, vc, kd, vd, qs, dos, e_buf, gp_buf,
    blk, st, dq_t, dqb, dqr, qlow, pin, pin_r,
    part, rec_r, rec_l, own,
    load_sem, st_ss, st_rs, dq_ss, dq_rs, in_ss, in_rs, sec_ss, r_rs, l_rs,
):
    sec = lax.axis_index("section")
    head = lax.axis_index("head")
    key = lax.axis_index("key")
    kvl, _, rows_c, _ = kd.shape
    group_rows = qs.shape[1]
    rows = q_v.shape[0]
    group = group_rows // rows
    blk_rows = kc.shape[0] // ke.shape[0]
    block_out = in_out.shape[0]
    scale = HD ** -0.5
    c0 = scale * LOG2E

    barrier = pltpu.get_barrier_semaphore()
    for d in range(1, n_key):
        pl.semaphore_signal(
            barrier, inc=1, device_id={"key": lax.rem(key + d, n_key)}, device_id_type=MESH
        )
    for d in range(1, n_head):
        pl.semaphore_signal(
            barrier, inc=1, device_id={"head": lax.rem(head + d, n_head)}, device_id_type=MESH
        )

    @pl.when(sec > 0)
    def _():
        pl.semaphore_signal(barrier, inc=1, device_id={"section": sec - 1}, device_id_type=MESH)

    @pl.when(sec < n_sec - 1)
    def _():
        pl.semaphore_signal(barrier, inc=1, device_id={"section": sec + 1}, device_id_type=MESH)

    loads = [
        pltpu.make_async_copy(src, dst, load_sem.at[i])
        for i, (src, dst) in enumerate(
            ((kc_hbm, kc), (q_hbm, q_v), (vc_hbm, vc), (do_hbm, do_v), (w_hbm, w_v))
        )
    ]
    for copy in loads:
        copy.start()

    def st_copy(d, g):
        return pltpu.make_async_remote_copy(
            src_ref=st.at[0, g], dst_ref=st.at[d, g],
            send_sem=st_ss.at[d, g], recv_sem=st_rs.at[d, g],
            device_id={"key": lax.rem(key + d, n_key)}, device_id_type=MESH,
        )

    def dq_copy(d, g):
        to = lax.rem(key + d, n_key)
        return pltpu.make_async_remote_copy(
            src_ref=dqb.at[g, to], dst_ref=dqr.at[d - 1, g],
            send_sem=dq_ss.at[d, g], recv_sem=dq_rs.at[d, g],
            device_id={"key": to}, device_id_type=MESH,
        )

    def in_copy(d):
        to = lax.rem(head + d, n_head)
        return pltpu.make_async_remote_copy(
            src_ref=pin.at[to], dst_ref=pin_r.at[d - 1],
            send_sem=in_ss.at[d], recv_sem=in_rs.at[d],
            device_id={"head": to}, device_id_type=MESH,
        )

    def right_copy(c, g):
        return pltpu.make_async_remote_copy(
            src_ref=part.at[c, g], dst_ref=rec_r.at[c, g],
            send_sem=sec_ss.at[c, g], recv_sem=r_rs.at[c, g],
            device_id={"section": jnp.minimum(sec + 1, n_sec - 1)}, device_id_type=MESH,
        )

    def left_copy(c, g):
        return pltpu.make_async_remote_copy(
            src_ref=part.at[c, g], dst_ref=rec_l.at[c, g],
            send_sem=sec_ss.at[c, g], recv_sem=l_rs.at[c, g],
            device_id={"section": jnp.maximum(sec - 1, 0)}, device_id_type=MESH,
        )

    def dequantize(codes, exps, out, g):
        for b in range(exps.shape[0]):
            first = b * blk_rows
            factor = lax.shift_left(jnp.int32(1), exps[b, g] + 16).astype(F32) * (2.0 ** -16)
            block = codes[first : first + blk_rows, g * HD : (g + 1) * HD].astype(F32) * factor
            at = first % rows_c
            out[g, first // rows_c, at : at + blk_rows, :] = block.astype(BF16)

    def stack_heads(src, out, g):
        for h in range(group):
            col = (g * group + h) * HD
            out[g, h * rows : (h + 1) * rows, :] = src[:, col : col + HD]

    def pass_one(g):
        slot = g % 2
        dequantize(kc, ke, kd, g)
        stack_heads(q_v, qs, g)
        if g == 0:
            loads[2].wait()
            loads[3].wait()
        dequantize(vc, ve, vd, g)
        stack_heads(do_v, dos, g)

        def step(c, carry):
            s = dot(kd[g, c], qs[g], NT)
            top = jnp.max(s, axis=0, keepdims=True)
            e = jnp.exp2((s - top) * c0)
            gp = dot(vd[g, c], dos[g], NT)
            e_buf[slot, c] = e
            gp_buf[slot, c] = gp
            blk[slot, c, 0:1, :] = top
            blk[slot, c, 1:2, :] = jnp.sum(e, axis=0, keepdims=True)
            blk[slot, c, 2:3, :] = jnp.sum(e * gp, axis=0, keepdims=True)
            return carry

        lax.fori_loop(0, n_sec, step, 0)
        tops = blk[slot, :, 0:1, :]
        top = jnp.max(tops, axis=0)
        weight = jnp.exp2((tops - top[None]) * c0)
        st[0, g, 0:1, :] = top
        st[0, g, 1:2, :] = jnp.sum(blk[slot, :, 1:2, :] * weight, axis=0)
        st[0, g, 2:3, :] = jnp.sum(blk[slot, :, 2:3, :] * weight, axis=0)
        st[0, g, 3:8, :] = jnp.zeros((5, group_rows), F32)
        if g == 0:
            beside = jnp.where(sec > 0, 1, 0) + jnp.where(sec < n_sec - 1, 1, 0)
            pl.semaphore_wait(barrier, n_key - 1 + n_head - 1 + beside)

        for d in range(1, n_key):
            st_copy(d, g).start()

    def pass_two(g):
        slot = g % 2
        for d in range(1, n_key):
            st_copy(d, g).wait_recv()
        tops = [st[d, g, 0:1, :] for d in range(n_key)]
        top = functools.reduce(jnp.maximum, tops)
        weights = [jnp.exp2((t - top) * c0) for t in tops]
        total = sum(st[d, g, 1:2, :] * weights[d] for d in range(n_key))
        inverse = 1.0 / total
        delta = sum(st[d, g, 2:3, :] * weights[d] for d in range(n_key)) * inverse
        dq_t[...] = jnp.zeros_like(dq_t)

        def step(t, carry):
            c = jnp.where(sec < n_sec // 2, n_sec - 1 - t, t)
            alpha = jnp.exp2((blk[slot, c, 0:1, :] - top) * c0) * inverse
            p = e_buf[slot, c] * alpha
            ds = (p * (gp_buf[slot, c] - delta)).astype(BF16)
            value_part = dot(p.astype(BF16), dos[g], NN)
            key_part = dot(ds, qs[g], NN) * scale
            dq_t[...] += dot(kd[g, c], ds, TN)

            @pl.when(c == sec)
            def _():
                own[g, 0] = key_part
                own[g, 1] = value_part

            @pl.when(c != sec)
            def _():
                part[c, g, 0] = key_part.astype(BF16)
                part[c, g, 1] = value_part.astype(BF16)

            @pl.when(jnp.logical_and(sec == 0, c > 0))
            def _():
                right_copy(c, g).start()

            @pl.when(jnp.logical_and(sec == n_sec - 1, c < n_sec - 1))
            def _():
                left_copy(c, g).start()

            return carry

        lax.fori_loop(0, n_sec, step, 0)
        dq = (jnp.transpose(dq_t[...]) * scale).astype(BF16)
        for k in range(n_key):
            for hh in range(n_head):
                for h in range(group):
                    first = h * rows + (hh * n_key + k) * block_out
                    dqb[g, k, hh * block_out : (hh + 1) * block_out, h * HD : (h + 1) * HD] = dq[
                        first : first + block_out
                    ]
        for d in range(1, n_key):
            dq_copy(d, g).start()

    def forward(g):
        def step(t, carry):
            right = n_sec - 1 - t

            @pl.when(jnp.logical_and(right > sec, sec > 0))
            def _():
                right_copy(right, g).wait_recv()
                part[right, g] = (
                    part[right, g].astype(F32) + rec_r[right, g].astype(F32)
                ).astype(BF16)
                right_copy(right, g).start()

            @pl.when(jnp.logical_and(t < sec, sec < n_sec - 1))
            def _():
                left_copy(t, g).wait_recv()
                part[t, g] = (part[t, g].astype(F32) + rec_l[t, g].astype(F32)).astype(BF16)
                left_copy(t, g).start()

            return carry

        lax.fori_loop(0, n_sec, step, 0)

    def finish(g):
        @pl.when(sec > 0)
        def _():
            right_copy(sec, g).wait_recv()
            own[g] += rec_r[sec, g].astype(F32)

        @pl.when(sec < n_sec - 1)
        def _():
            left_copy(sec, g).wait_recv()
            own[g] += rec_l[sec, g].astype(F32)

        key_out[:, g * HD : (g + 1) * HD] = own[g, 0]
        value_out[:, g * HD : (g + 1) * HD] = own[g, 1]

    loads[0].wait()
    loads[1].wait()
    pass_one(0)
    for g in range(1, kvl):
        pass_one(g)
        pass_two(g - 1)
    pass_two(kvl - 1)
    forward(0)

    width = group * HD
    for g in range(kvl):
        for d in range(1, n_key):
            dq_copy(d, g).wait_recv()
        total = dqb[g, key].astype(F32)
        for d in range(1, n_key):
            total = total + dqr[d - 1, g].astype(F32)
        qlow[:, g * width : (g + 1) * width] = total.astype(BF16)
    loads[4].wait()
    wide = w_v.shape[0]
    tile = 512

    def columns(i, carry):
        first = pl.multiple_of(i * tile, tile)
        product = dot(qlow[...], w_v[pl.ds(first, tile), :], NT).astype(BF16)
        for hh in range(n_head):
            pin[hh, :, pl.ds(first, tile)] = product[hh * block_out : (hh + 1) * block_out]
        return carry

    lax.fori_loop(0, wide // tile, columns, 0)
    for d in range(1, n_head):
        in_copy(d).start()

    finish(0)
    for g in range(1, kvl):
        forward(g)
        finish(g)

    for d in range(1, n_head):
        in_copy(d).wait_recv()
    total = pin[head].astype(F32)
    for d in range(1, n_head):
        total = total + pin_r[d - 1].astype(F32)
    in_out[...] = total.astype(BF16)

    for g in range(kvl):
        for d in range(1, n_key):
            st_copy(d, g).wait_send()
            dq_copy(d, g).wait_send()

        def drain(c, carry, g=g):
            @pl.when(c > sec)
            def _():
                right_copy(c, g).wait_send()

            @pl.when(c < sec)
            def _():
                left_copy(c, g).wait_send()

            return carry

        lax.fori_loop(0, n_sec, drain, 0)
    for d in range(1, n_head):
        in_copy(d).wait_send()


def body(n_sec, n_head, n_key, queries, attn_grad, query_weight, kc, ke, vc, ve):
    rows, cols = queries.shape[1:]
    wide = query_weight.shape[1]
    positions, kv_cols = kc.shape
    kvl = kv_cols // HD
    group_rows = cols // kv_cols * rows
    rows_c = positions // n_sec
    block_out = rows // (n_head * n_key)
    group_cols = cols // kvl
    vmem = pltpu.VMEM
    dma = pltpu.SemaphoreType.DMA
    anywhere = pl.BlockSpec(memory_space=pl.ANY)
    scalars = pl.BlockSpec(memory_space=pltpu.SMEM)
    in_vmem = pl.BlockSpec(memory_space=pltpu.VMEM)
    input_grad, key_grad, value_grad = pl.pallas_call(
        functools.partial(kernel, n_sec, n_head, n_key),
        out_shape=(
            jax.ShapeDtypeStruct((block_out, wide), BF16),
            jax.ShapeDtypeStruct((rows_c, kv_cols), F32),
            jax.ShapeDtypeStruct((rows_c, kv_cols), F32),
        ),
        in_specs=[anywhere, anywhere, anywhere, anywhere, scalars, anywhere, scalars],
        out_specs=(in_vmem, in_vmem, in_vmem),
        scratch_shapes=[
            vmem((rows, cols), BF16),
            vmem((rows, cols), BF16),
            vmem((wide, cols), BF16),
            vmem((positions, kv_cols), jnp.int32),
            vmem((positions, kv_cols), jnp.int32),
            vmem((kvl, n_sec, rows_c, HD), BF16),
            vmem((kvl, n_sec, rows_c, HD), BF16),
            vmem((kvl, group_rows, HD), BF16),
            vmem((kvl, group_rows, HD), BF16),
            vmem((2, n_sec, rows_c, group_rows), F32),
            vmem((2, n_sec, rows_c, group_rows), F32),
            vmem((2, n_sec, 8, group_rows), F32),
            vmem((n_key, kvl, 8, group_rows), F32),
            vmem((HD, group_rows), F32),
            vmem((kvl, n_key, n_head * block_out, group_cols), BF16),
            vmem((n_key - 1, kvl, n_head * block_out, group_cols), BF16),
            vmem((n_head * block_out, cols), BF16),
            vmem((n_head, block_out, wide), BF16),
            vmem((n_head - 1, block_out, wide), BF16),
            vmem((n_sec, kvl, 2, rows_c, HD), BF16),
            vmem((n_sec, kvl, 2, rows_c, HD), BF16),
            vmem((n_sec, kvl, 2, rows_c, HD), BF16),
            vmem((kvl, 2, rows_c, HD), F32),
            dma((5,)),
            dma((n_key, kvl)),
            dma((n_key, kvl)),
            dma((n_key, kvl)),
            dma((n_key, kvl)),
            dma((n_head,)),
            dma((n_head,)),
            dma((n_sec, kvl)),
            dma((n_sec, kvl)),
            dma((n_sec, kvl)),
        ],
        compiler_params=pltpu.CompilerParams(
            collective_id=0, has_side_effects=True, vmem_limit_bytes=58 * 1024 * 1024
        ),
    )(queries[0], attn_grad[0], query_weight[0], kc, ke, vc, ve)
    return input_grad[None], key_grad, value_grad


def solution(mesh):
    shape = mesh.shape
    return jax.shard_map(
        functools.partial(body, shape["section"], shape["head"], shape["key"]),
        mesh=mesh,
        in_specs=(
            P("section", None, "head"),
            P("section", None, "head"),
            P("section", None, "head"),
            P("key", "head"),
            P("key", "head"),
            P("key", "head"),
            P("key", "head"),
        ),
        out_specs=(
            P("section", ("head", "key"), None),
            P(("key", "section"), "head"),
            P(("key", "section"), "head"),
        ),
        check_vma=False,
    )
```

time: 238 us -> 79.7 us (0.33)
  waiting for transfers between devices: 92.8 us -> 0 us
  Pallas kernels: 0 us -> 70.6 us
  matrix products: 43.6 us -> 0 us
  blocking collectives: 34.2 us -> 0 us
  other arithmetic: 23.9 us -> 0 us
  local copies, waits for them, and re-layouts: 26.3 us -> 8.06 us
  between operations: 16 us -> 0.64 us
    reduce_scatter x5 -> x0, waiting for transfers between devices: 83.7 us -> none  [the longest x2 54.1 us: body(): lax.psum_scatter(key_part.astype(jnp.bfloat16), 'section', scatter_dimens...]
    pallas_call x0 -> x1, Pallas kernels: none -> 70.6 us  [body(): pl.pallas_call(functools.partial(kernel, n_sec, n_head, n_key), out_shape...]
    dot_general x11 -> x0, matrix products: 43.6 us -> none  [the longest x2 12 us: body(): jnp.einsum('rkgd,skd->kgrs', grad_tick, value_vals, preferred_element_typ...]
    all_gather x4 -> x0, blocking collectives: 22 us -> none  [combined_all(): pieces = jax.tree.map(lambda part: lax.all_gather(part, axis), value)]
    convert_element_type x3 -> x0, other arithmetic: 16.2 us -> none  [the longest x1 12.8 us: body(): grads_low = grad_scores.astype(jnp.bfloat16)]
    psum x1 -> x0, blocking collectives: 12.3 us -> none  [body(): row_delta = lax.psum(jnp.sum(prob_full * grad_probs, axis=-1), 'key')]
    unnamed x7 -> x0, waiting for transfers between devices: 9.06 us -> none
    convert_element_type x4 -> x0, local copies, waits for them, and re-layouts: 8.43 us -> none  [the longest x2 4.61 us: body(): key_part.astype(jnp.bfloat16)]
  transfers between devices with their start and end apart: 6 -> 0, of which waited for: 5 -> 0; matrix products, arithmetic and copies ran while one was open for 16% -> 0% of each run, Pallas kernels for 0% -> 0%
where the time goes in v1:
time: 79.7 us; the launch traced here: 79.3 us
  Pallas kernels  70.6 us (89%)
  local copies, waits for them, and re-layouts  8.06 us (10%)
    pallas_call x1, Pallas kernels, body(): pl.pallas_call(functools.partial(kernel, n_sec, n_head, n_key), out_shape...  70.6 us
    unnamed x5, local copies, waits for them, and re-layouts  8.06 us

profile of v1, /device:TPU:0, one launch (start us, length us, event | category | flops | bytes accessed | tf_op | source)
XLA Modules:
  0.0 79.3 jit_solution(6601958497464789830)
XLA Ops:
  0.6 1.4 %copy.10.ke = s32[16,4]{1,0:T(8,128)} copy(s32[16,4]{0,1:T(4,128)} %param.11) | data formatting | bytes 512 | tf_op args[4]
  2.0 1.4 %copy.11.ve = s32[16,4]{1,0:T(8,128)} copy(s32[16,4]{0,1:T(4,128)} %param.13) | data formatting | bytes 512 | tf_op args[6]
  3.3 70.6 %shard_map.94 = (bf16[32,3072]{1,0:T(8,128)(2,1)}, f32[256,512]{1,0:T(8,128)}, f32[256,512]{1,0:T(8,128)}) custom-call(bf16[256,1536]{1,0:T(8,128)(2,1)} %bitcast.5, bf16[256,1536]{1,0:T(8,128)(2,1)} %bitcast.6, bf16[3072,1536]{1,0:T(8,128)(2,1)} %bitcast.4, s32[1024,512]{1,0:T(8,128)} %kc_hbm.1, s32[16,4]{1,0:T(8,128)} %copy.10.ke, s32[1024,512]{1,0:T(8,128)} %vc_hbm.1, ...), custom_call_target="tpu_custom_call" | custom-call | tf_op jit(solution)/shard_map/pallas_call | solution.py:327
  74.0 1.6 %copy.15 = bf16[1,32,3072]{2,1,0:T(8,128)(2,1)} copy(bf16[1,32,3072]{2,1,0:T(8,128)(2,1)} %bitcast.7) | data formatting | bytes 393216
  75.6 1.9 %copy.16 = f32[256,512]{1,0:T(8,128)} copy(f32[256,512]{1,0:T(8,128)} %get-tuple-element.13) | data formatting | bytes 1048576
  77.5 1.9 %copy.17 = f32[256,512]{1,0:T(8,128)} copy(f32[256,512]{1,0:T(8,128)} %get-tuple-element.14) | data formatting | bytes 1048576

commit v2 on v1

--- a/solution.py
+++ b/solution.py
@@ -23,21 +23,21 @@
 
 def kernel(
     n_sec, n_head, n_key,
-    q_hbm, do_hbm, w_hbm, kc_hbm, ke, vc_hbm, ve,
+    q_hbm, do_hbm, w_hbm, kc_hbm, ke_hbm, vc_hbm, ve_hbm,
     in_out, key_out, value_out,
-    q_v, do_v, w_v, kc, vc, kd, vd, qs, dos, e_buf, gp_buf,
+    ke, ve, w_v, kc, vc, kd, vd, qs, dos, e_buf, gp_buf,
     blk, st, dq_t, dqb, dqr, qlow, pin, pin_r,
     part, rec_r, rec_l, own,
-    load_sem, st_ss, st_rs, dq_ss, dq_rs, in_ss, in_rs, sec_ss, r_rs, l_rs,
+    exp_sem, code_sem, row_sem, w_sem, st_ss, st_rs, dq_ss, dq_rs, in_ss, in_rs, sec_ss, r_rs, l_rs,
 ):
     sec = lax.axis_index("section")
     head = lax.axis_index("head")
     key = lax.axis_index("key")
     kvl, _, rows_c, _ = kd.shape
     group_rows = qs.shape[1]
-    rows = q_v.shape[0]
+    rows = q_hbm.shape[0]
     group = group_rows // rows
-    blk_rows = kc.shape[0] // ke.shape[0]
+    blk_rows = kc.shape[0] // ke.shape[1]
     block_out = in_out.shape[0]
     scale = HD ** -0.5
     c0 = scale * LOG2E
@@ -60,14 +60,31 @@
     def _():
         pl.semaphore_signal(barrier, inc=1, device_id={"section": sec + 1}, device_id_type=MESH)
 
-    loads = [
-        pltpu.make_async_copy(src, dst, load_sem.at[i])
-        for i, (src, dst) in enumerate(
-            ((kc_hbm, kc), (q_hbm, q_v), (vc_hbm, vc), (do_hbm, do_v), (w_hbm, w_v))
-        )
+    def code_load(i, g):
+        src, dst = ((kc_hbm, kc), (vc_hbm, vc))[i]
+        cols = pl.ds(g * HD, HD)
+        return pltpu.make_async_copy(src.at[:, cols], dst.at[:, cols], code_sem.at[i, g])
+
+    def row_load(i, g, h):
+        src, dst = ((q_hbm, qs), (do_hbm, dos))[i]
+        return pltpu.make_async_copy(
+            src.at[:, pl.ds((g * group + h) * HD, HD)],
+            dst.at[g, pl.ds(h * rows, rows)],
+            row_sem.at[i, g, h],
+        )
+
+    exp_loads = [
+        pltpu.make_async_copy(ke_hbm, ke, exp_sem.at[0]),
+        pltpu.make_async_copy(ve_hbm, ve, exp_sem.at[1]),
     ]
-    for copy in loads:
+    w_load = pltpu.make_async_copy(w_hbm, w_v, w_sem)
+    for copy in exp_loads:
         copy.start()
+    for g in range(kvl):
+        for i in range(2):
+            code_load(i, g).start()
+            for h in range(group):
+                row_load(i, g, h).start()
 
     def st_copy(d, g):
         return pltpu.make_async_remote_copy(
@@ -107,27 +124,24 @@
         )
 
     def dequantize(codes, exps, out, g):
-        for b in range(exps.shape[0]):
+        factors = lax.shift_left(jnp.int32(1), exps[...] + 16).astype(F32) * (2.0 ** -16)
+        for b in range(exps.shape[1]):
             first = b * blk_rows
-            factor = lax.shift_left(jnp.int32(1), exps[b, g] + 16).astype(F32) * (2.0 ** -16)
-            block = codes[first : first + blk_rows, g * HD : (g + 1) * HD].astype(F32) * factor
+            block = codes[first : first + blk_rows, g * HD : (g + 1) * HD].astype(F32)
             at = first % rows_c
-            out[g, first // rows_c, at : at + blk_rows, :] = block.astype(BF16)
-
-    def stack_heads(src, out, g):
-        for h in range(group):
-            col = (g * group + h) * HD
-            out[g, h * rows : (h + 1) * rows, :] = src[:, col : col + HD]
+            out[g, first // rows_c, at : at + blk_rows, :] = (
+                block * factors[g : g + 1, b : b + 1]
+            ).astype(BF16)
 
     def pass_one(g):
         slot = g % 2
-        dequantize(kc, ke, kd, g)
-        stack_heads(q_v, qs, g)
-        if g == 0:
-            loads[2].wait()
-            loads[3].wait()
-        dequantize(vc, ve, vd, g)
-        stack_heads(do_v, dos, g)
+        for i, (codes, exps, out) in enumerate(((kc, ke, kd), (vc, ve, vd))):
+            if g == 0:
+                exp_loads[i].wait()
+            code_load(i, g).wait()
+            dequantize(codes, exps, out, g)
+            for h in range(group):
+                row_load(i, g, h).wait()
 
         def step(c, carry):
             s = dot(kd[g, c], qs[g], NT)
@@ -152,6 +166,7 @@
         if g == 0:
             beside = jnp.where(sec > 0, 1, 0) + jnp.where(sec < n_sec - 1, 1, 0)
             pl.semaphore_wait(barrier, n_key - 1 + n_head - 1 + beside)
+            w_load.start()
 
         for d in range(1, n_key):
             st_copy(d, g).start()
@@ -209,23 +224,29 @@
         for d in range(1, n_key):
             dq_copy(d, g).start()
 
-    def forward(g):
+    def relay(stage):
+        inner = jnp.logical_and(sec > 0, sec < n_sec - 1)
+        right_g, left_g = stage - sec, stage - (n_sec - 1 - sec)
+        right_on = jnp.logical_and(inner, jnp.logical_and(right_g >= 0, right_g < kvl))
+        left_on = jnp.logical_and(inner, jnp.logical_and(left_g >= 0, left_g < kvl))
+        rg, lg = jnp.clip(right_g, 0, kvl - 1), jnp.clip(left_g, 0, kvl - 1)
+
         def step(t, carry):
             right = n_sec - 1 - t
 
-            @pl.when(jnp.logical_and(right > sec, sec > 0))
-            def _():
-                right_copy(right, g).wait_recv()
-                part[right, g] = (
-                    part[right, g].astype(F32) + rec_r[right, g].astype(F32)
+            @pl.when(jnp.logical_and(right > sec, right_on))
+            def _():
+                right_copy(right, rg).wait_recv()
+                part[right, rg] = (
+                    part[right, rg].astype(F32) + rec_r[right, rg].astype(F32)
                 ).astype(BF16)
-                right_copy(right, g).start()
-
-            @pl.when(jnp.logical_and(t < sec, sec < n_sec - 1))
-            def _():
-                left_copy(t, g).wait_recv()
-                part[t, g] = (part[t, g].astype(F32) + rec_l[t, g].astype(F32)).astype(BF16)
-                left_copy(t, g).start()
+                right_copy(right, rg).start()
+
+            @pl.when(jnp.logical_and(t < sec, left_on))
+            def _():
+                left_copy(t, lg).wait_recv()
+                part[t, lg] = (part[t, lg].astype(F32) + rec_l[t, lg].astype(F32)).astype(BF16)
+                left_copy(t, lg).start()
 
             return carry
 
@@ -245,14 +266,14 @@
         key_out[:, g * HD : (g + 1) * HD] = own[g, 0]
         value_out[:, g * HD : (g + 1) * HD] = own[g, 1]
 
-    loads[0].wait()
-    loads[1].wait()
     pass_one(0)
     for g in range(1, kvl):
         pass_one(g)
         pass_two(g - 1)
+        if g > 1:
+            relay(g - 1)
     pass_two(kvl - 1)
-    forward(0)
+    relay(kvl - 1)
 
     width = group * HD
     for g in range(kvl):
@@ -262,7 +283,7 @@
         for d in range(1, n_key):
             total = total + dqr[d - 1, g].astype(F32)
         qlow[:, g * width : (g + 1) * width] = total.astype(BF16)
-    loads[4].wait()
+    w_load.wait()
     wide = w_v.shape[0]
     tile = 512
 
@@ -273,13 +294,15 @@
             pin[hh, :, pl.ds(first, tile)] = product[hh * block_out : (hh + 1) * block_out]
         return carry
 
-    lax.fori_loop(0, wide // tile, columns, 0)
+    half = wide // tile // 2
+    lax.fori_loop(0, half, columns, 0)
+    relay(kvl)
+    lax.fori_loop(half, wide // tile, columns, 0)
     for d in range(1, n_head):
         in_copy(d).start()
-
-    finish(0)
-    for g in range(1, kvl):
-        forward(g)
+    for stage in range(kvl + 1, kvl + n_sec - 2):
+        relay(stage)
+    for g in range(kvl):
         finish(g)
 
     for d in range(1, n_head):
@@ -308,6 +331,17 @@
         lax.fori_loop(0, n_sec, drain, 0)
     for d in range(1, n_head):
         in_copy(d).wait_send()
+
+
+def hand_out(a, b, c, a_out, b_out, c_out, sem):
+    copies = [
+        pltpu.make_async_copy(src, dst, sem.at[i])
+        for i, (src, dst) in enumerate(((a, a_out), (b, b_out), (c, c_out)))
+    ]
+    for copy in copies:
+        copy.start()
+    for copy in copies:
+        copy.wait()
 
 
 def body(n_sec, n_head, n_key, queries, attn_grad, query_weight, kc, ke, vc, ve):
@@ -322,20 +356,19 @@
     vmem = pltpu.VMEM
     dma = pltpu.SemaphoreType.DMA
     anywhere = pl.BlockSpec(memory_space=pl.ANY)
-    scalars = pl.BlockSpec(memory_space=pltpu.SMEM)
     in_vmem = pl.BlockSpec(memory_space=pltpu.VMEM)
-    input_grad, key_grad, value_grad = pl.pallas_call(
+    results = pl.pallas_call(
         functools.partial(kernel, n_sec, n_head, n_key),
         out_shape=(
             jax.ShapeDtypeStruct((block_out, wide), BF16),
             jax.ShapeDtypeStruct((rows_c, kv_cols), F32),
             jax.ShapeDtypeStruct((rows_c, kv_cols), F32),
         ),
-        in_specs=[anywhere, anywhere, anywhere, anywhere, scalars, anywhere, scalars],
+        in_specs=[anywhere] * 7,
         out_specs=(in_vmem, in_vmem, in_vmem),
         scratch_shapes=[
-            vmem((rows, cols), BF16),
-            vmem((rows, cols), BF16),
+            vmem(ke.T.shape, jnp.int32),
+            vmem(ve.T.shape, jnp.int32),
             vmem((wide, cols), BF16),
             vmem((positions, kv_cols), jnp.int32),
             vmem((positions, kv_cols), jnp.int32),
@@ -357,7 +390,10 @@
             vmem((n_sec, kvl, 2, rows_c, HD), BF16),
             vmem((n_sec, kvl, 2, rows_c, HD), BF16),
             vmem((kvl, 2, rows_c, HD), F32),
-            dma((5,)),
+            dma((2,)),
+            dma((2, kvl)),
+            dma((2, kvl, cols // kv_cols)),
+            dma,
             dma((n_key, kvl)),
             dma((n_key, kvl)),
             dma((n_key, kvl)),
@@ -371,7 +407,15 @@
         compiler_params=pltpu.CompilerParams(
             collective_id=0, has_side_effects=True, vmem_limit_bytes=58 * 1024 * 1024
         ),
-    )(queries[0], attn_grad[0], query_weight[0], kc, ke, vc, ve)
+    )(queries[0], attn_grad[0], query_weight[0], kc, ke.T, vc, ve.T)
+    input_grad, key_grad, value_grad = pl.pallas_call(
+        hand_out,
+        out_shape=tuple(jax.ShapeDtypeStruct(r.shape, r.dtype) for r in results),
+        in_specs=[anywhere] * 3,
+        out_specs=(anywhere,) * 3,
+        scratch_shapes=[dma((3,))],
+        compiler_params=pltpu.CompilerParams(vmem_limit_bytes=62 * 1024 * 1024),
+    )(*results)
     return input_grad[None], key_grad, value_grad
 
 

time: 79.7 us -> 92.3 us (1.16)
  Pallas kernels: 70.6 us -> 91.6 us
  local copies, waits for them, and re-layouts: 8.06 us -> 0 us
    pallas_call x0 -> x1, Pallas kernels: none -> 38.9 us  [body(): pl.pallas_call(hand_out, out_shape=tuple((jax.ShapeDtypeStruct(r.shape, r...]
    pallas_call x1, Pallas kernels: 70.6 us -> 52.7 us  [body(): pl.pallas_call(functools.partial(kernel, n_sec, n_head, n_key), out_shape...]
    unnamed x5 -> x0, local copies, waits for them, and re-layouts: 8.06 us -> none
where the time goes in v2:
time: 92.3 us; the launch traced here: 92.2 us
  Pallas kernels  91.6 us (99%)
    pallas_call x1, Pallas kernels, body(): pl.pallas_call(functools.partial(kernel, n_sec, n_head, n_key), out_shape...  52.7 us
    pallas_call x1, Pallas kernels, body(): pl.pallas_call(hand_out, out_shape=tuple((jax.ShapeDtypeStruct(r.shape, r...  38.9 us

profile of v2, /device:TPU:0, one launch (start us, length us, event | category | flops | bytes accessed | tf_op | source)
XLA Modules:
  0.0 92.2 jit_solution(9190597018470514851)
XLA Ops:
  0.6 52.7 %shard_map.94 = (bf16[32,3072]{1,0:T(8,128)(2,1)}, f32[256,512]{1,0:T(8,128)}, f32[256,512]{1,0:T(8,128)}) custom-call(bf16[256,1536]{1,0:T(8,128)(2,1)} %bitcast.7, bf16[256,1536]{1,0:T(8,128)(2,1)} %bitcast.8, bf16[3072,1536]{1,0:T(8,128)(2,1)} %bitcast.6, s32[1024,512]{1,0:T(8,128)} %kc_hbm.1, s32[4,16]{1,0:T(4,128)} %bitcast.9, s32[1024,512]{1,0:T(8,128)} %vc_hbm.1, ...), custom_call_target="tpu_custom_call" | custom-call | tf_op jit(solution)/shard_map/pallas_call | solution.py:360
  53.3 38.9 %shard_map.95 = (bf16[32,3072]{1,0:T(8,128)(2,1)}, f32[256,512]{1,0:T(8,128)}, f32[256,512]{1,0:T(8,128)}) custom-call(bf16[32,3072]{1,0:T(8,128)(2,1)} %get-tuple-element.9.a, f32[256,512]{1,0:T(8,128)} %get-tuple-element.10.b, f32[256,512]{1,0:T(8,128)} %get-tuple-element.11.c), custom_call_target="tpu_custom_call" | custom-call | tf_op jit(solution)/shard_map/pallas_call | solution.py:411

commit v3 on v2

--- a/solution.py
+++ b/solution.py
@@ -133,8 +133,7 @@
                 block * factors[g : g + 1, b : b + 1]
             ).astype(BF16)
 
-    def pass_one(g):
-        slot = g % 2
+    def unpack(g):
         for i, (codes, exps, out) in enumerate(((kc, ke, kd), (vc, ve, vd))):
             if g == 0:
                 exp_loads[i].wait()
@@ -143,16 +142,22 @@
             for h in range(group):
                 row_load(i, g, h).wait()
 
+    def pass_one(g):
+        slot = g % 2
+
         def step(c, carry):
-            s = dot(kd[g, c], qs[g], NT)
-            top = jnp.max(s, axis=0, keepdims=True)
-            e = jnp.exp2((s - top) * c0)
-            gp = dot(vd[g, c], dos[g], NT)
-            e_buf[slot, c] = e
-            gp_buf[slot, c] = gp
-            blk[slot, c, 0:1, :] = top
-            blk[slot, c, 1:2, :] = jnp.sum(e, axis=0, keepdims=True)
-            blk[slot, c, 2:3, :] = jnp.sum(e * gp, axis=0, keepdims=True)
+            keys, values = kd[g, c], vd[g, c]
+            for h in range(group):
+                cols = slice(h * rows, (h + 1) * rows)
+                s = dot(keys, qs[g, cols], NT)
+                gp = dot(values, dos[g, cols], NT)
+                top = jnp.max(s, axis=0, keepdims=True)
+                e = jnp.exp2((s - top) * c0)
+                e_buf[slot, c, :, cols] = e
+                gp_buf[slot, c, :, cols] = gp
+                blk[slot, c, 0:1, cols] = top
+                blk[slot, c, 1:2, cols] = jnp.sum(e, axis=0, keepdims=True)
+                blk[slot, c, 2:3, cols] = jnp.sum(e * gp, axis=0, keepdims=True)
             return carry
 
         lax.fori_loop(0, n_sec, step, 0)
@@ -266,14 +271,18 @@
         key_out[:, g * HD : (g + 1) * HD] = own[g, 0]
         value_out[:, g * HD : (g + 1) * HD] = own[g, 1]
 
+    unpack(0)
     pass_one(0)
     for g in range(1, kvl):
-        pass_one(g)
-        pass_two(g - 1)
-        if g > 1:
-            relay(g - 1)
-    pass_two(kvl - 1)
-    relay(kvl - 1)
+        unpack(g)
+    pass_two(0)
+    if kvl > 1:
+        pass_one(1)
+    for g in range(1, kvl):
+        if g + 1 < kvl:
+            pass_one(g + 1)
+        pass_two(g)
+        relay(g)
 
     width = group * HD
     for g in range(kvl):
@@ -333,14 +342,16 @@
         in_copy(d).wait_send()
 
 
-def hand_out(a, b, c, a_out, b_out, c_out, sem):
-    copies = [
-        pltpu.make_async_copy(src, dst, sem.at[i])
-        for i, (src, dst) in enumerate(((a, a_out), (b, b_out), (c, c_out)))
-    ]
-    for copy in copies:
+def hand_out(*refs):
+    ins, outs, held, sem = refs[:3], refs[3:6], refs[6:9], refs[9]
+    come = [pltpu.make_async_copy(ins[i], held[i], sem.at[0, i]) for i in range(3)]
+    leave = [pltpu.make_async_copy(held[i], outs[i], sem.at[1, i]) for i in range(3)]
+    for copy in come:
         copy.start()
-    for copy in copies:
+    for i in range(3):
+        come[i].wait()
+        leave[i].start()
+    for copy in leave:
         copy.wait()
 
 
@@ -413,7 +424,7 @@
         out_shape=tuple(jax.ShapeDtypeStruct(r.shape, r.dtype) for r in results),
         in_specs=[anywhere] * 3,
         out_specs=(anywhere,) * 3,
-        scratch_shapes=[dma((3,))],
+        scratch_shapes=[vmem(r.shape, r.dtype) for r in results] + [dma((2, 3))],
         compiler_params=pltpu.CompilerParams(vmem_limit_bytes=62 * 1024 * 1024),
     )(*results)
     return input_grad[None], key_grad, value_grad

time: 92.3 us -> 55.8 us (0.60)
  Pallas kernels: 91.6 us -> 55 us
    pallas_call x1, Pallas kernels: 38.9 us -> 2.17 us  [body(): pl.pallas_call(hand_out, out_shape=tuple((jax.ShapeDtypeStruct(r.shape, r...]
where the time goes in v3:
time: 55.8 us; the launch traced here: 55.6 us
  Pallas kernels  55 us (99%)
  between operations  0.64 us (1%)
    pallas_call x1, Pallas kernels, body(): pl.pallas_call(functools.partial(kernel, n_sec, n_head, n_key), out_shape...  52.8 us
    pallas_call x1, Pallas kernels, body(): pl.pallas_call(hand_out, out_shape=tuple((jax.ShapeDtypeStruct(r.shape, r...  2.17 us

profile of v3, /device:TPU:0, one launch (start us, length us, event | category | flops | bytes accessed | tf_op | source)
XLA Modules:
  0.0 55.6 jit_solution(10075248569006656303)
XLA Ops:
  0.6 52.8 %shard_map.94 = (bf16[32,3072]{1,0:T(8,128)(2,1)}, f32[256,512]{1,0:T(8,128)}, f32[256,512]{1,0:T(8,128)}) custom-call(bf16[256,1536]{1,0:T(8,128)(2,1)} %bitcast.7, bf16[256,1536]{1,0:T(8,128)(2,1)} %bitcast.8, bf16[3072,1536]{1,0:T(8,128)(2,1)} %bitcast.6, s32[1024,512]{1,0:T(8,128)} %kc_hbm.1, s32[4,16]{1,0:T(4,128)} %bitcast.9, s32[1024,512]{1,0:T(8,128)} %vc_hbm.1, ...), custom_call_target="tpu_custom_call" | custom-call | tf_op jit(solution)/shard_map/pallas_call | solution.py:371
  53.5 2.2 %shard_map.95 = (bf16[32,3072]{1,0:T(8,128)(2,1)}, f32[256,512]{1,0:T(8,128)}, f32[256,512]{1,0:T(8,128)}) custom-call(bf16[32,3072]{1,0:T(8,128)(2,1)} %get-tuple-element.9.refs_0_, f32[256,512]{1,0:T(8,128)} %get-tuple-element.10.refs_1_, f32[256,512]{1,0:T(8,128)} %get-tuple-element.11.refs_2_), custom_call_target="tpu_custom_call" | custom-call | tf_op jit(solution)/shard_map/pallas_call | solution.py:422

commit v4 on v3

--- a/solution.py
+++ b/solution.py
@@ -142,10 +142,26 @@
             for h in range(group):
                 row_load(i, g, h).wait()
 
+    def by_chunks(most, work, after=None):
+        several = most if n_sec % most == 0 else 1
+
+        def step(i, carry):
+            for u in range(several):
+                work(i * several + u)
+            if after is not None:
+                for u in range(several):
+                    after(i * several + u)
+            return carry
+
+        if several == n_sec:
+            step(0, 0)
+        else:
+            lax.fori_loop(0, n_sec // several, step, 0)
+
     def pass_one(g):
         slot = g % 2
 
-        def step(c, carry):
+        def chunk(c):
             keys, values = kd[g, c], vd[g, c]
             for h in range(group):
                 cols = slice(h * rows, (h + 1) * rows)
@@ -158,9 +174,8 @@
                 blk[slot, c, 0:1, cols] = top
                 blk[slot, c, 1:2, cols] = jnp.sum(e, axis=0, keepdims=True)
                 blk[slot, c, 2:3, cols] = jnp.sum(e * gp, axis=0, keepdims=True)
-            return carry
-
-        lax.fori_loop(0, n_sec, step, 0)
+
+        by_chunks(4, chunk)
         tops = blk[slot, :, 0:1, :]
         top = jnp.max(tops, axis=0)
         weight = jnp.exp2((tops - top[None]) * c0)
@@ -188,24 +203,22 @@
         delta = sum(st[d, g, 2:3, :] * weights[d] for d in range(n_key)) * inverse
         dq_t[...] = jnp.zeros_like(dq_t)
 
-        def step(t, carry):
-            c = jnp.where(sec < n_sec // 2, n_sec - 1 - t, t)
+        def place(t):
+            return jnp.where(sec < n_sec // 2, n_sec - 1 - t, t)
+
+        def chunk(t):
+            c = place(t)
             alpha = jnp.exp2((blk[slot, c, 0:1, :] - top) * c0) * inverse
             p = e_buf[slot, c] * alpha
             ds = (p * (gp_buf[slot, c] - delta)).astype(BF16)
             value_part = dot(p.astype(BF16), dos[g], NN)
             key_part = dot(ds, qs[g], NN) * scale
             dq_t[...] += dot(kd[g, c], ds, TN)
-
-            @pl.when(c == sec)
-            def _():
-                own[g, 0] = key_part
-                own[g, 1] = value_part
-
-            @pl.when(c != sec)
-            def _():
-                part[c, g, 0] = key_part.astype(BF16)
-                part[c, g, 1] = value_part.astype(BF16)
+            part[c, g, 0] = key_part.astype(BF16)
+            part[c, g, 1] = value_part.astype(BF16)
+
+        def send(t):
+            c = place(t)
 
             @pl.when(jnp.logical_and(sec == 0, c > 0))
             def _():
@@ -215,9 +228,7 @@
             def _():
                 left_copy(c, g).start()
 
-            return carry
-
-        lax.fori_loop(0, n_sec, step, 0)
+        by_chunks(2, chunk, send)
         dq = (jnp.transpose(dq_t[...]) * scale).astype(BF16)
         for k in range(n_key):
             for hh in range(n_head):
@@ -258,18 +269,20 @@
         lax.fori_loop(0, n_sec, step, 0)
 
     def finish(g):
+        own[...] = part[sec, g].astype(F32)
+
         @pl.when(sec > 0)
         def _():
             right_copy(sec, g).wait_recv()
-            own[g] += rec_r[sec, g].astype(F32)
+            own[...] += rec_r[sec, g].astype(F32)
 
         @pl.when(sec < n_sec - 1)
         def _():
             left_copy(sec, g).wait_recv()
-            own[g] += rec_l[sec, g].astype(F32)
-
-        key_out[:, g * HD : (g + 1) * HD] = own[g, 0]
-        value_out[:, g * HD : (g + 1) * HD] = own[g, 1]
+            own[...] += rec_l[sec, g].astype(F32)
+
+        key_out[:, g * HD : (g + 1) * HD] = own[0]
+        value_out[:, g * HD : (g + 1) * HD] = own[1]
 
     unpack(0)
     pass_one(0)
@@ -400,7 +413,7 @@
             vmem((n_sec, kvl, 2, rows_c, HD), BF16),
             vmem((n_sec, kvl, 2, rows_c, HD), BF16),
             vmem((n_sec, kvl, 2, rows_c, HD), BF16),
-            vmem((kvl, 2, rows_c, HD), F32),
+            vmem((2, rows_c, HD), F32),
             dma((2,)),
             dma((2, kvl)),
             dma((2, kvl, cols // kv_cols)),

time: 55.8 us -> 55.4 us (level)
  no operation moved by 1% of the time
where the time goes in v4:
time: 55.4 us; the launch traced here: 55.2 us
  Pallas kernels  54.6 us (99%)
  between operations  0.64 us (1%)
    pallas_call x1, Pallas kernels, body(): pl.pallas_call(functools.partial(kernel, n_sec, n_head, n_key), out_shape...  52.4 us
    pallas_call x1, Pallas kernels, body(): pl.pallas_call(hand_out, out_shape=tuple((jax.ShapeDtypeStruct(r.shape, r...  2.17 us

profile of v4, /device:TPU:0, one launch (start us, length us, event | category | flops | bytes accessed | tf_op | source)
XLA Modules:
  0.0 55.2 jit_solution(13611987183619290208)
XLA Ops:
  0.6 52.4 %shard_map.94 = (bf16[32,3072]{1,0:T(8,128)(2,1)}, f32[256,512]{1,0:T(8,128)}, f32[256,512]{1,0:T(8,128)}) custom-call(bf16[256,1536]{1,0:T(8,128)(2,1)} %bitcast.7, bf16[256,1536]{1,0:T(8,128)(2,1)} %bitcast.8, bf16[3072,1536]{1,0:T(8,128)(2,1)} %bitcast.6, s32[1024,512]{1,0:T(8,128)} %kc_hbm.1, s32[4,16]{1,0:T(4,128)} %bitcast.9, s32[1024,512]{1,0:T(8,128)} %vc_hbm.1, ...), custom_call_target="tpu_custom_call" | custom-call | tf_op jit(solution)/shard_map/pallas_call | solution.py:384
  53.1 2.2 %shard_map.95 = (bf16[32,3072]{1,0:T(8,128)(2,1)}, f32[256,512]{1,0:T(8,128)}, f32[256,512]{1,0:T(8,128)}) custom-call(bf16[32,3072]{1,0:T(8,128)(2,1)} %get-tuple-element.9.refs_0_, f32[256,512]{1,0:T(8,128)} %get-tuple-element.10.refs_1_, f32[256,512]{1,0:T(8,128)} %get-tuple-element.11.refs_2_), custom_call_target="tpu_custom_call" | custom-call | tf_op jit(solution)/shard_map/pallas_call | solution.py:435

commit v5 on v4

--- a/solution.py
+++ b/solution.py
@@ -27,8 +27,8 @@
     in_out, key_out, value_out,
     ke, ve, w_v, kc, vc, kd, vd, qs, dos, e_buf, gp_buf,
     blk, st, dq_t, dqb, dqr, qlow, pin, pin_r,
-    part, rec_r, rec_l, own,
-    exp_sem, code_sem, row_sem, w_sem, st_ss, st_rs, dq_ss, dq_rs, in_ss, in_rs, sec_ss, r_rs, l_rs,
+    part, rec_r, rec_l, own, h_q, h_do, h_st, h_st_out,
+    exp_sem, code_sem, row_sem, w_sem, st_ss, st_rs, dq_ss, dq_rs, in_ss, in_rs, sec_ss, r_rs, l_rs, h_ss, h_rs,
 ):
     sec = lax.axis_index("section")
     head = lax.axis_index("head")
@@ -41,6 +41,9 @@
     block_out = in_out.shape[0]
     scale = HD ** -0.5
     c0 = scale * LOG2E
+    shared = kvl - 1 if n_sec >= 4 else -1
+    ends = jnp.logical_or(sec == 0, sec == n_sec - 1)
+    helpers = jnp.logical_or(sec == 1, sec == n_sec - 2)
 
     barrier = pltpu.get_barrier_semaphore()
     for d in range(1, n_key):
@@ -84,7 +87,17 @@
         for i in range(2):
             code_load(i, g).start()
             for h in range(group):
-                row_load(i, g, h).start()
+                if g == 0 or g != shared:
+                    row_load(i, g, h).start()
+                if g == 0 and shared > 0:
+                    row_load(i, shared, h).start()
+
+    def help_copy(i):
+        src, dst = ((qs.at[shared], h_q), (dos.at[shared], h_do), (h_st_out, h_st))[i]
+        return pltpu.make_async_remote_copy(
+            src_ref=src, dst_ref=dst, send_sem=h_ss.at[i], recv_sem=h_rs.at[i],
+            device_id={"section": jnp.where(sec == 0, 1, n_sec - 2)}, device_id_type=MESH,
+        )
 
     def st_copy(d, g):
         return pltpu.make_async_remote_copy(
@@ -140,7 +153,10 @@
             code_load(i, g).wait()
             dequantize(codes, exps, out, g)
             for h in range(group):
-                row_load(i, g, h).wait()
+                if g == 0 or g != shared:
+                    row_load(i, g, h).wait()
+                if g == 0 and shared > 0:
+                    row_load(i, shared, h).wait()
 
     def by_chunks(most, work, after=None):
         several = most if n_sec % most == 0 else 1
@@ -183,11 +199,6 @@
         st[0, g, 1:2, :] = jnp.sum(blk[slot, :, 1:2, :] * weight, axis=0)
         st[0, g, 2:3, :] = jnp.sum(blk[slot, :, 2:3, :] * weight, axis=0)
         st[0, g, 3:8, :] = jnp.zeros((5, group_rows), F32)
-        if g == 0:
-            beside = jnp.where(sec > 0, 1, 0) + jnp.where(sec < n_sec - 1, 1, 0)
-            pl.semaphore_wait(barrier, n_key - 1 + n_head - 1 + beside)
-            w_load.start()
-
         for d in range(1, n_key):
             st_copy(d, g).start()
 
@@ -201,6 +212,16 @@
         total = sum(st[d, g, 1:2, :] * weights[d] for d in range(n_key))
         inverse = 1.0 / total
         delta = sum(st[d, g, 2:3, :] * weights[d] for d in range(n_key)) * inverse
+        if g == shared:
+
+            @pl.when(ends)
+            def _():
+                h_st_out[0:1] = top
+                h_st_out[1:2] = inverse
+                h_st_out[2:3] = delta
+                h_st_out[3:8] = jnp.zeros((5, group_rows), F32)
+                help_copy(2).start()
+
         dq_t[...] = jnp.zeros_like(dq_t)
 
         def place(t):
@@ -228,7 +249,7 @@
             def _():
                 left_copy(c, g).start()
 
-        by_chunks(2, chunk, send)
+        by_chunks(2, chunk, None if g == shared else send)
         dq = (jnp.transpose(dq_t[...]) * scale).astype(BF16)
         for k in range(n_key):
             for hh in range(n_head):
@@ -252,17 +273,48 @@
 
             @pl.when(jnp.logical_and(right > sec, right_on))
             def _():
-                right_copy(right, rg).wait_recv()
-                part[right, rg] = (
-                    part[right, rg].astype(F32) + rec_r[right, rg].astype(F32)
-                ).astype(BF16)
+                @pl.when(jnp.logical_not(jnp.logical_and(sec == 1, rg == shared)))
+                def _():
+                    right_copy(right, rg).wait_recv()
+                    part[right, rg] = (
+                        part[right, rg].astype(F32) + rec_r[right, rg].astype(F32)
+                    ).astype(BF16)
+
                 right_copy(right, rg).start()
 
             @pl.when(jnp.logical_and(t < sec, left_on))
             def _():
-                left_copy(t, lg).wait_recv()
-                part[t, lg] = (part[t, lg].astype(F32) + rec_l[t, lg].astype(F32)).astype(BF16)
+                @pl.when(jnp.logical_not(jnp.logical_and(sec == n_sec - 2, lg == shared)))
+                def _():
+                    left_copy(t, lg).wait_recv()
+                    part[t, lg] = (part[t, lg].astype(F32) + rec_l[t, lg].astype(F32)).astype(BF16)
+
                 left_copy(t, lg).start()
+
+            return carry
+
+        lax.fori_loop(0, n_sec, step, 0)
+
+    def assist():
+        for i in range(3):
+            help_copy(i).wait_recv()
+        top, inverse, delta = h_st[0:1], h_st[1:2], h_st[2:3]
+
+        def step(c, carry):
+            @pl.when(jnp.where(sec == 1, c > 0, c < n_sec - 1))
+            def _():
+                key_part = part[c, shared, 0].astype(F32)
+                value_part = part[c, shared, 1].astype(F32)
+                for h in range(group):
+                    cols = slice(h * rows, (h + 1) * rows)
+                    s = dot(kd[shared, c], h_q[cols], NT)
+                    gp = dot(vd[shared, c], h_do[cols], NT)
+                    p = jnp.exp2((s - top[:, cols]) * c0) * inverse[:, cols]
+                    ds = (p * (gp - delta[:, cols])).astype(BF16)
+                    key_part += dot(ds, h_q[cols], NN) * scale
+                    value_part += dot(p.astype(BF16), h_do[cols], NN)
+                part[c, shared, 0] = key_part.astype(BF16)
+                part[c, shared, 1] = value_part.astype(BF16)
 
             return carry
 
@@ -271,12 +323,17 @@
     def finish(g):
         own[...] = part[sec, g].astype(F32)
 
-        @pl.when(sec > 0)
+        from_left, from_right = sec > 0, sec < n_sec - 1
+        if g == shared:
+            from_left = jnp.logical_and(from_left, sec != 1)
+            from_right = jnp.logical_and(from_right, sec != n_sec - 2)
+
+        @pl.when(from_left)
         def _():
             right_copy(sec, g).wait_recv()
             own[...] += rec_r[sec, g].astype(F32)
 
-        @pl.when(sec < n_sec - 1)
+        @pl.when(from_right)
         def _():
             left_copy(sec, g).wait_recv()
             own[...] += rec_l[sec, g].astype(F32)
@@ -285,6 +342,16 @@
         value_out[:, g * HD : (g + 1) * HD] = own[1]
 
     unpack(0)
+    beside = jnp.where(sec > 0, 1, 0) + jnp.where(sec < n_sec - 1, 1, 0)
+    pl.semaphore_wait(barrier, n_key - 1 + n_head - 1 + beside)
+    if shared >= 0:
+
+        @pl.when(ends)
+        def _():
+            help_copy(0).start()
+            help_copy(1).start()
+
+    w_load.start()
     pass_one(0)
     for g in range(1, kvl):
         unpack(g)
@@ -296,6 +363,8 @@
             pass_one(g + 1)
         pass_two(g)
         relay(g)
+    if shared >= 0:
+        pl.when(helpers)(assist)
 
     width = group * HD
     for g in range(kvl):
@@ -340,11 +409,16 @@
             dq_copy(d, g).wait_send()
 
         def drain(c, carry, g=g):
-            @pl.when(c > sec)
+            to_right, to_left = c > sec, c < sec
+            if g == shared:
+                to_right = jnp.logical_and(to_right, sec != 0)
+                to_left = jnp.logical_and(to_left, sec != n_sec - 1)
+
+            @pl.when(to_right)
             def _():
                 right_copy(c, g).wait_send()
 
-            @pl.when(c < sec)
+            @pl.when(to_left)
             def _():
                 left_copy(c, g).wait_send()
 
@@ -353,6 +427,12 @@
         lax.fori_loop(0, n_sec, drain, 0)
     for d in range(1, n_head):
         in_copy(d).wait_send()
+    if shared >= 0:
+
+        @pl.when(ends)
+        def _():
+            for i in range(3):
+                help_copy(i).wait_send()
 
 
 def hand_out(*refs):
@@ -414,6 +494,10 @@
             vmem((n_sec, kvl, 2, rows_c, HD), BF16),
             vmem((n_sec, kvl, 2, rows_c, HD), BF16),
             vmem((2, rows_c, HD), F32),
+            vmem((group_rows, HD), BF16),
+            vmem((group_rows, HD), BF16),
+            vmem((8, group_rows), F32),
+            vmem((8, group_rows), F32),
             dma((2,)),
             dma((2, kvl)),
             dma((2, kvl, cols // kv_cols)),
@@ -427,6 +511,8 @@
             dma((n_sec, kvl)),
             dma((n_sec, kvl)),
             dma((n_sec, kvl)),
+            dma((3,)),
+            dma((3,)),
         ],
         compiler_params=pltpu.CompilerParams(
             collective_id=0, has_side_effects=True, vmem_limit_bytes=58 * 1024 * 1024

time: 55.4 us -> 61.2 us (1.10)
  Pallas kernels: 54.6 us -> 60.4 us
    pallas_call x1, Pallas kernels: 52.4 us -> 58.2 us  [body(): pl.pallas_call(functools.partial(kernel, n_sec, n_head, n_key), out_shape...]
where the time goes in v5:
time: 61.2 us; the launch traced here: 61.1 us
  Pallas kernels  60.4 us (99%)
  between operations  0.64 us (1%)
    pallas_call x1, Pallas kernels, body(): pl.pallas_call(functools.partial(kernel, n_sec, n_head, n_key), out_shape...  58.2 us
    pallas_call x1, Pallas kernels, body(): pl.pallas_call(hand_out, out_shape=tuple((jax.ShapeDtypeStruct(r.shape, r...  2.17 us

profile of v5, /device:TPU:0, one launch (start us, length us, event | category | flops | bytes accessed | tf_op | source)
XLA Modules:
  0.0 61.1 jit_solution(7879089202108889637)
XLA Ops:
  0.6 58.2 %shard_map.94 = (bf16[32,3072]{1,0:T(8,128)(2,1)}, f32[256,512]{1,0:T(8,128)}, f32[256,512]{1,0:T(8,128)}) custom-call(bf16[256,1536]{1,0:T(8,128)(2,1)} %bitcast.7, bf16[256,1536]{1,0:T(8,128)(2,1)} %bitcast.8, bf16[3072,1536]{1,0:T(8,128)(2,1)} %bitcast.6, s32[1024,512]{1,0:T(8,128)} %kc_hbm.1, s32[4,16]{1,0:T(4,128)} %bitcast.9, s32[1024,512]{1,0:T(8,128)} %vc_hbm.1, ...), custom_call_target="tpu_custom_call" | custom-call | tf_op jit(solution)/shard_map/pallas_call | solution.py:464
  58.9 2.2 %shard_map.95 = (bf16[32,3072]{1,0:T(8,128)(2,1)}, f32[256,512]{1,0:T(8,128)}, f32[256,512]{1,0:T(8,128)}) custom-call(bf16[32,3072]{1,0:T(8,128)(2,1)} %get-tuple-element.9.refs_0_, f32[256,512]{1,0:T(8,128)} %get-tuple-element.10.refs_1_, f32[256,512]{1,0:T(8,128)} %get-tuple-element.11.refs_2_), custom_call_target="tpu_custom_call" | custom-call | tf_op jit(solution)/shard_map/pallas_call | solution.py:521

commit v6 on v5

--- a/solution.py
+++ b/solution.py
@@ -266,6 +266,8 @@
         right_g, left_g = stage - sec, stage - (n_sec - 1 - sec)
         right_on = jnp.logical_and(inner, jnp.logical_and(right_g >= 0, right_g < kvl))
         left_on = jnp.logical_and(inner, jnp.logical_and(left_g >= 0, left_g < kvl))
+        right_on = jnp.logical_and(right_on, jnp.logical_or(sec != 1, right_g != shared))
+        left_on = jnp.logical_and(left_on, jnp.logical_or(sec != n_sec - 2, left_g != shared))
         rg, lg = jnp.clip(right_g, 0, kvl - 1), jnp.clip(left_g, 0, kvl - 1)
 
         def step(t, carry):
@@ -273,22 +275,16 @@
 
             @pl.when(jnp.logical_and(right > sec, right_on))
             def _():
-                @pl.when(jnp.logical_not(jnp.logical_and(sec == 1, rg == shared)))
-                def _():
-                    right_copy(right, rg).wait_recv()
-                    part[right, rg] = (
-                        part[right, rg].astype(F32) + rec_r[right, rg].astype(F32)
-                    ).astype(BF16)
-
+                right_copy(right, rg).wait_recv()
+                part[right, rg] = (
+                    part[right, rg].astype(F32) + rec_r[right, rg].astype(F32)
+                ).astype(BF16)
                 right_copy(right, rg).start()
 
             @pl.when(jnp.logical_and(t < sec, left_on))
             def _():
-                @pl.when(jnp.logical_not(jnp.logical_and(sec == n_sec - 2, lg == shared)))
-                def _():
-                    left_copy(t, lg).wait_recv()
-                    part[t, lg] = (part[t, lg].astype(F32) + rec_l[t, lg].astype(F32)).astype(BF16)
-
+                left_copy(t, lg).wait_recv()
+                part[t, lg] = (part[t, lg].astype(F32) + rec_l[t, lg].astype(F32)).astype(BF16)
                 left_copy(t, lg).start()
 
             return carry
@@ -316,6 +312,14 @@
                 part[c, shared, 0] = key_part.astype(BF16)
                 part[c, shared, 1] = value_part.astype(BF16)
 
+                @pl.when(jnp.logical_and(sec == 1, c > 1))
+                def _():
+                    right_copy(c, shared).start()
+
+                @pl.when(jnp.logical_and(sec == n_sec - 2, c < n_sec - 2))
+                def _():
+                    left_copy(c, shared).start()
+
             return carry
 
         lax.fori_loop(0, n_sec, step, 0)
@@ -361,8 +365,11 @@
     for g in range(1, kvl):
         if g + 1 < kvl:
             pass_one(g + 1)
+        if g < kvl - 1:
+            relay(g - 1)
         pass_two(g)
-        relay(g)
+    if kvl > 1:
+        relay(kvl - 2)
     if shared >= 0:
         pl.when(helpers)(assist)
 
@@ -387,11 +394,11 @@
 
     half = wide // tile // 2
     lax.fori_loop(0, half, columns, 0)
-    relay(kvl)
+    relay(kvl - 1)
     lax.fori_loop(half, wide // tile, columns, 0)
     for d in range(1, n_head):
         in_copy(d).start()
-    for stage in range(kvl + 1, kvl + n_sec - 2):
+    for stage in range(kvl, kvl + n_sec - 2):
         relay(stage)
     for g in range(kvl):
         finish(g)

time: 61.2 us -> 64.6 us (1.056)
  Pallas kernels: 60.4 us -> 63.8 us
    pallas_call x1, Pallas kernels: 58.2 us -> 61.6 us  [body(): pl.pallas_call(functools.partial(kernel, n_sec, n_head, n_key), out_shape...]
where the time goes in v6:
time: 64.6 us; the launch traced here: 64.4 us
  Pallas kernels  63.8 us (99%)
    pallas_call x1, Pallas kernels, body(): pl.pallas_call(functools.partial(kernel, n_sec, n_head, n_key), out_shape...  61.6 us
    pallas_call x1, Pallas kernels, body(): pl.pallas_call(hand_out, out_shape=tuple((jax.ShapeDtypeStruct(r.shape, r...  2.17 us

profile of v6, /device:TPU:0, one launch (start us, length us, event | category | flops | bytes accessed | tf_op | source)
XLA Modules:
  0.0 64.4 jit_solution(13085272503275654454)
XLA Ops:
  0.6 61.6 %shard_map.94 = (bf16[32,3072]{1,0:T(8,128)(2,1)}, f32[256,512]{1,0:T(8,128)}, f32[256,512]{1,0:T(8,128)}) custom-call(bf16[256,1536]{1,0:T(8,128)(2,1)} %bitcast.7, bf16[256,1536]{1,0:T(8,128)(2,1)} %bitcast.8, bf16[3072,1536]{1,0:T(8,128)(2,1)} %bitcast.6, s32[1024,512]{1,0:T(8,128)} %kc_hbm.1, s32[4,16]{1,0:T(4,128)} %bitcast.9, s32[1024,512]{1,0:T(8,128)} %vc_hbm.1, ...), custom_call_target="tpu_custom_call" | custom-call | tf_op jit(solution)/shard_map/pallas_call | solution.py:471
  62.3 2.2 %shard_map.95 = (bf16[32,3072]{1,0:T(8,128)(2,1)}, f32[256,512]{1,0:T(8,128)}, f32[256,512]{1,0:T(8,128)}) custom-call(bf16[32,3072]{1,0:T(8,128)(2,1)} %get-tuple-element.9.refs_0_, f32[256,512]{1,0:T(8,128)} %get-tuple-element.10.refs_1_, f32[256,512]{1,0:T(8,128)} %get-tuple-element.11.refs_2_), custom_call_target="tpu_custom_call" | custom-call | tf_op jit(solution)/shard_map/pallas_call | solution.py:528
